TPU v7x, 128 devices: a whole 4x4x4 slice. The times are simulated.
128 devices in a mesh: loader: 4 (over z_hi, core), centers: 32 (over y, z_lo, x).
Axes of the slice: x: 4, y: 4, z: 4 (z_hi: 2, z_lo: 2; z = z_hi * 2 + z_lo), core: 2. Of those that a mesh axis runs over, the one named last changes fastest.
Arguments:
- pool: bfloat16 [32768, 256], P('loader'), may hold values from -6 to 6
- batch_index: int32 [2048], replicated, may hold values from 0 to 32767
- targets: float32 [16, 2048], replicated, may hold values from -6 to 6
- centers: bfloat16 [1048576, 256], P(('loader', 'centers')), may hold values from -6 to 6
- weights: float32 [16, 1048576], P(None, ('loader', 'centers')), may hold values from -1.8 to 1.8
- nys_index: int32 [8192], P(('loader', 'centers')), may hold values from 0 to 8191, as said below
- eigvecs: float32 [8192, 128], P(('loader', 'centers')), may hold values from -0.0625 to 0.0625
- damping: float32 [128], replicated, may hold values from 1 to 30
Outputs:
- new_weights: float32 [16, 1048576], P(None, ('loader', 'centers'))
- predictions: float32 [16, 2048], replicated
Inputs may be any that keep to these rules, and one draw needn't show every extreme that they name: `nys_index`: each device's block of 64 entries names distinct local rows of that device's own 8192 centers; entry k lies in [k * 128, (k + 1) * 128); the first is 0 and the last 8191.
All inputs are finite; a program needn't handle non-finite values.
Results may differ from a plain program's by a relative error of at most 0.0049.
Values may be sent and summed in bfloat16 or wider, within the bound.
No kernel may reach another device: no remote copies, remote signals or barrier semaphores. Data moves between devices by JAX's collectives and lax.ppermute only.
A program may use at most 256 MiB of HBM per device.

v0:
```python
import math
import jax
import jax.numpy as jnp
from jax import lax
from jax.sharding import PartitionSpec as P

D = 256


def pick_rows(pool, wanted):
    held = pool.shape[0]
    local = wanted - lax.axis_index("loader") * held
    owned = (local >= 0) & (local < held)
    rows = pool[jnp.clip(local, 0, held - 1)]
    return jnp.where(owned[:, None], rows, jnp.zeros_like(rows))


def body(pool, batch_index, targets, centers, weights, nys_index, eigvecs, damping):
    total_rows = batch_index.shape[0]
    share = total_rows // lax.axis_size("centers")
    mine = lax.dynamic_slice_in_dim(batch_index, lax.axis_index("centers") * share, share)
    summed = lax.psum(pick_rows(pool, mine), "loader").astype(jnp.float32).astype(jnp.bfloat16)
    batch = lax.all_gather(summed, "centers", axis=0, tiled=True)
    cen_sq = jnp.sum(centers.astype(jnp.float32) * centers.astype(jnp.float32), axis=1)
    width = min(512, total_rows)

    def tile(rows):
        row_sq = jnp.sum(rows.astype(jnp.float32) * rows.astype(jnp.float32), axis=1)
        cross = jnp.dot(rows, centers.T, preferred_element_type=jnp.float32)
        dist_sq = row_sq[:, None] + cen_sq[None, :] - 2.0 * cross
        return jnp.exp(-4.0 * jnp.sqrt(dist_sq) / math.sqrt(D)).astype(jnp.bfloat16)

    kern = lax.map(tile, batch.reshape(total_rows // width, width, batch.shape[1]))
    kern = kern.reshape(total_rows, centers.shape[0])
    w_half = weights.astype(jnp.bfloat16)
    partial_value = lax.dot_general(
        w_half, kern, (((1,), (1,)), ((), ())), preferred_element_type=jnp.float32
    )
    predictions = lax.psum(partial_value, ("loader", "centers"))
    resid = (predictions - targets).astype(jnp.bfloat16)
    grad = jnp.dot(resid, kern, preferred_element_type=jnp.float32)
    grad_nys = grad[:, nys_index]
    local_coeff = jnp.dot(
        grad_nys, eigvecs, precision=lax.Precision.HIGHEST, preferred_element_type=jnp.float32
    )
    coeff = lax.psum(local_coeff, ("loader", "centers"))
    delta = jnp.dot(
        coeff * damping[None, :],
        eigvecs.T,
        precision=lax.Precision.HIGHEST,
        preferred_element_type=jnp.float32,
    )
    fresh = weights - 2.0 * grad
    fresh = fresh.at[:, nys_index].add(2.0 * delta)
    return (fresh, predictions)


def solution(mesh):
    return jax.shard_map(
        body,
        mesh=mesh,
        in_specs=(
            P("loader", None),
            P(),
            P(),
            P(("loader", "centers"), None),
            P(None, ("loader", "centers")),
            P(("loader", "centers")),
            P(("loader", "centers"), None),
            P(),
        ),
        out_specs=(P(None, ("loader", "centers")), P()),
        check_vma=False,
    )
```

profile of v0, /device:TPU:1, one launch (start us, length us, event | category | flops | bytes accessed | tf_op | source)
XLA Modules:
  0.0 498.1 jit_solution(4399989665971109694)
XLA Ops:
  7.2 0.0 all-gather.2.cloned.1.call-start
  7.2 0.8 compare_select_fusion.1
  8.0 0.8 compare_and_fusion
  8.8 3.4 gather_fusion
  12.2 0.1 broadcast_select_fusion
  12.2 15.6 %psum.21 = bf16[64,256]{1,0:T(8,128)(2,1)} all-reduce(bf16[64,256]{1,0:T(8,128)(2,1)S(1)} %broadcast_select_fusion), channel_id=1, replica_groups=mesh['loader'=4,'centers'=32] {'loader'}, use_global_device_ids=true, to_apply=%region_0.1 | all-reduce | flops 16384 | bytes 65536 | tf_op jit(solution)/shard_map/psum | solution.py:22
  27.9 0.0 all-reduce.2.cloned.1.call-start
  28.0 0.7 compare_select_fusion
  28.6 3.3 multiply_reduce_fusion.1
  32.0 127.5 %all-gather.2.cloned.1.call-done = bf16[2048,256]{1,0:T(8,128)(2,1)} async-done(((bf16[64,256]{1,0:T(8,128)(2,1)}), bf16[2048,256]{1,0:T(8,128)(2,1)}) %all-gather.2.cloned.1.call-update) | async-done | bytes 1048592 | tf_op jit(solution)/shard_map/all_gather | solution.py:23
  159.5 58.4 %while.12 = (s32[]{:T(128)}, bf16[4,512,8192]{2,1,0:T(8,128)(2,1)}, bf16[4,512,256]{2,1,0:T(8,128)(2,1)}, f32[8192]{0:T(1024)S(1)}, bf16[8192,256]{1,0:T(8,128)(2,1)}, /*index=5*/s32[]{:T(128)}) while((s32[]{:T(128)}, bf16[4,512,8192]{2,1,0:T(8,128)(2,1)}, bf16[4,512,256]{2,1,0:T(8,128)(2,1)}, f32[8192]{0:T(1024)S(1)}, ...), condition=%wide.region_4.5_spmd, body=%wide.region_2.4_spmd.sunk | while | flops 2168847872 | bytes 13145161 | solution.py:33
  159.5 1.2 multiply_reduce_fusion.3
  160.6 13.5 %fusion.22 = bf16[4,512,8192]{2,1,0:T(8,128)(2,1)} fusion(bf16[4,512,8192]{2,1,0:T(8,128)(2,1)} %get-tuple-element.120, s32[]{:T(128)} %get-tuple-element.119, bf16[8192,256]{1,0:T(8,128)(2,1)} %get-tuple-element.129, f32[8192]{0:T(1024)S(1)} %get-tuple-element.128, f32[512]{0:T(512)S(1)} %multiply_reduce_fusion.3, ...), kind=kOutput, calls=%fused_computation.5.clone.1 | convolution fusion | flops 2168455168 | bytes 12880896 | tf_op jit(solution)/shard_map/while/body/eval_jaxpr/dot_general | solution.py:29
  174.1 1.1 multiply_reduce_fusion.3
  175.2 13.5 %fusion.22 = bf16[4,512,8192]{2,1,0:T(8,128)(2,1)} fusion(bf16[4,512,8192]{2,1,0:T(8,128)(2,1)} %get-tuple-element.120, s32[]{:T(128)} %get-tuple-element.119, bf16[8192,256]{1,0:T(8,128)(2,1)} %get-tuple-element.129, f32[8192]{0:T(1024)S(1)} %get-tuple-element.128, f32[512]{0:T(512)S(1)} %multiply_reduce_fusion.3, ...), kind=kOutput, calls=%fused_computation.5.clone.1 | convolution fusion | flops 2168455168 | bytes 12880896 | tf_op jit(solution)/shard_map/while/body/eval_jaxpr/dot_general | solution.py:29
  188.7 1.1 multiply_reduce_fusion.3
  189.8 13.5 %fusion.22 = bf16[4,512,8192]{2,1,0:T(8,128)(2,1)} fusion(bf16[4,512,8192]{2,1,0:T(8,128)(2,1)} %get-tuple-element.120, s32[]{:T(128)} %get-tuple-element.119, bf16[8192,256]{1,0:T(8,128)(2,1)} %get-tuple-element.129, f32[8192]{0:T(1024)S(1)} %get-tuple-element.128, f32[512]{0:T(512)S(1)} %multiply_reduce_fusion.3, ...), kind=kOutput, calls=%fused_computation.5.clone.1 | convolution fusion | flops 2168455168 | bytes 12880896 | tf_op jit(solution)/shard_map/while/body/eval_jaxpr/dot_general | solution.py:29
  203.3 1.1 multiply_reduce_fusion.3
  204.4 13.5 %fusion.22 = bf16[4,512,8192]{2,1,0:T(8,128)(2,1)} fusion(bf16[4,512,8192]{2,1,0:T(8,128)(2,1)} %get-tuple-element.120, s32[]{:T(128)} %get-tuple-element.119, bf16[8192,256]{1,0:T(8,128)(2,1)} %get-tuple-element.129, f32[8192]{0:T(1024)S(1)} %get-tuple-element.128, f32[512]{0:T(512)S(1)} %multiply_reduce_fusion.3, ...), kind=kOutput, calls=%fused_computation.5.clone.1 | convolution fusion | flops 2168455168 | bytes 12880896 | tf_op jit(solution)/shard_map/while/body/eval_jaxpr/dot_general | solution.py:29
  217.9 15.7 %convolution_bitcast_fusion = f32[16,2048]{1,0:T(8,128)} fusion(bf16[2048,8192]{1,0:T(8,128)(2,1)} %bitcast.28, f32[16,8192]{1,0:T(8,128)S(1)} %copy-done.1), kind=kOutput, calls=%fused_computation.11 | convolution fusion | flops 537001984 | bytes 34209792 | tf_op jit(solution)/shard_map/dot_general | solution.py:36
  233.6 161.8 %all-reduce.2.cloned.1.call-done = f32[16,2048]{1,0:T(8,128)} async-done(((f32[16,2048]{1,0:T(8,128)}), f32[16,2048]{1,0:T(8,128)}) %all-reduce.2.cloned.1.call-update) | async-done | bytes 131088 | tf_op jit(solution)/shard_map/psum | solution.py:39
  395.4 14.8 %multiply_subtract_fusion = (f32[16,8192]{1,0:T(8,128)S(1)}, f32[16,8192]{1,0:T(8,128)S(1)}) fusion(f32[16,8192]{1,0:T(8,128)S(1)} %copy-done.1, bf16[2048,8192]{1,0:T(8,128)(2,1)} %bitcast.29, f32[16,2048]{1,0:T(8,128)} %all-reduce.2.cloned.1.call-done, f32[16,2048]{1,0:T(8,128)S(1)} %copy-done.3), kind=kOutput, calls=%fused_computation.14 | convolution fusion | flops 537198592 | bytes 35389440 | tf_op jit(solution)/shard_map/dot_general | solution.py:41
  410.3 2.6 copy.10
  412.9 2.8 gather_fusion.1
  415.7 0.2 fusion.10
  415.9 63.4 %psum.23 = f32[16,128]{1,0:T(8,128)S(1)} all-reduce(f32[16,128]{1,0:T(8,128)S(1)} %fusion.10), channel_id=1, replica_groups=mesh['loader'=4,'centers'=32] {'loader','centers'}, use_global_device_ids=true, to_apply=%region_6.7 | all-reduce | flops 2048 | bytes 16384 | tf_op jit(solution)/shard_map/psum | solution.py:46
  479.3 0.1 fusion.5
  479.4 0.1 copy.12
  479.5 2.6 copy.11
  482.1 4.9 scatter_fusion
  487.1 3.5 copy.13
  490.6 0.7 copy.25
  (15 shorter events, 0.1 us)
Async XLA Ops:
  7.2 408.5 %copy-start = (f32[64,128]{1,0:T(8,128)S(1)}, f32[64,128]{1,0:T(8,128)}, u32[]{:S(2)}) copy-start(f32[64,128]{1,0:T(8,128)} %param.16) | copy-start | bytes 98308
  7.2 152.3 %all-gather.2.cloned.1.call-start = ((), (), s32[]{:S(2)}) async-start(), calls=%async_computation | async-start | bytes 1081344 | tf_op jit(solution)/shard_map/all_gather | solution.py:23
  27.9 367.5 %all-reduce.2.cloned.1.call-start = ((), (), s32[]{:S(2)}) async-start(), calls=%async_computation.1 | async-start | bytes 262144 | tf_op jit(solution)/shard_map/psum | solution.py:39
  159.5 58.4 %copy-start.1 = (f32[16,8192]{1,0:T(8,128)S(1)}, f32[16,8192]{1,0:T(8,128)}, u32[]{:S(2)}) copy-start(f32[16,8192]{1,0:T(8,128)} %param.14) | copy-start | bytes 1572868
  217.9 177.5 %copy-start.3 = (f32[16,2048]{1,0:T(8,128)S(1)}, f32[16,2048]{1,0:T(8,128)}, u32[]{:S(2)}) copy-start(f32[16,2048]{1,0:T(8,128)} %param.12) | copy-start | bytes 393220
  233.6 245.7 %copy-start.4 = (f32[128]{0:T(128)S(1)}, f32[128]{0:T(128)}, u32[]{:S(2)}) copy-start(f32[128]{0:T(128)} %param.17) | copy-start | bytes 1540
  395.4 95.2 %copy-start.2 = (f32[16,2048]{1,0:T(8,128)S(1)}, f32[16,2048]{1,0:T(8,128)}, u32[]{:S(2)}) copy-start(f32[16,2048]{1,0:T(8,128)} %all-reduce.2.cloned.1.call-done) | copy-start | bytes 393220
Sparse Core Ops, SparseCore 0:
  28.0 131.4 all-gather.1
  233.7 161.6 all-reduce.1
where the time goes:
time: 499 us; the launch traced here: 498 us
  waiting for transfers between devices  289 us (58%)
  matrix products  84.8 us (17%)
  blocking collectives  79.1 us (16%)
  local copies, waits for them, and re-layouts  15.7 us (3%)
  other arithmetic  15 us (3%)
  between operations  14.1 us (3%)
    psum x1, waiting for transfers between devices, body(): predictions = lax.psum(partial_value, ('loader', 'centers'))  162 us
    all_gather x1, waiting for transfers between devices, body(): batch = lax.all_gather(summed, 'centers', axis=0, tiled=True)  128 us
    psum x1, blocking collectives, body(): coeff = lax.psum(local_coeff, ('loader', 'centers'))  63.4 us
    dot_general x4, matrix products, tile(): cross = jnp.dot(rows, centers.T, preferred_element_type=jnp.float32)  54 us
    dot_general x1, matrix products, body(): lax.dot_general(w_half, kern, (((1,), (1,)), ((), ())), preferred_element...  15.7 us
    psum x1, blocking collectives, body(): lax.psum(pick_rows(pool, mine), 'loader').astype(jnp.float32)  15.6 us
    dot_general x1, matrix products, body(): grad = jnp.dot(resid, kern, preferred_element_type=jnp.float32)  14.8 us
  transfers between devices with their start and end apart: 2, of which 2 were waited for; matrix products, arithmetic and copies ran while one was open for 1% of the time, Pallas kernels for 0%

commit v1 on v0

--- a/solution.py
+++ b/solution.py
@@ -43,7 +43,7 @@
     local_coeff = jnp.dot(
         grad_nys, eigvecs, precision=lax.Precision.HIGHEST, preferred_element_type=jnp.float32
     )
-    coeff = lax.psum(local_coeff, ("loader", "centers"))
+    coeff = lax.psum(lax.psum(local_coeff, "centers"), "loader")
     delta = jnp.dot(
         coeff * damping[None, :],
         eigvecs.T,

time: 499 us -> 523 us (1.048)
  blocking collectives: 79.1 us -> 103 us
    psum x1 -> x2, blocking collectives: 63.4 us -> 87.6 us  [body(): coeff = lax.psum(lax.psum(local_coeff, 'centers'), 'loader')]
where the time goes in v1:
time: 523 us; the launch traced here: 522 us
  waiting for transfers between devices  289 us (55%)
  blocking collectives  103 us (20%)
  matrix products  84.8 us (16%)
  local copies, waits for them, and re-layouts  15.7 us (3%)
  other arithmetic  15 us (3%)
  between operations  14.1 us (3%)
    psum x1, waiting for transfers between devices, body(): predictions = lax.psum(partial_value, ('loader', 'centers'))  162 us
    all_gather x1, waiting for transfers between devices, body(): batch = lax.all_gather(summed, 'centers', axis=0, tiled=True)  128 us
    psum x2, blocking collectives, body(): coeff = lax.psum(lax.psum(local_coeff, 'centers'), 'loader')  87.6 us
    dot_general x4, matrix products, tile(): cross = jnp.dot(rows, centers.T, preferred_element_type=jnp.float32)  54 us
    dot_general x1, matrix products, body(): lax.dot_general(w_half, kern, (((1,), (1,)), ((), ())), preferred_element...  15.7 us
    psum x1, blocking collectives, body(): lax.psum(pick_rows(pool, mine), 'loader').astype(jnp.float32)  15.6 us
    dot_general x1, matrix products, body(): grad = jnp.dot(resid, kern, preferred_element_type=jnp.float32)  14.8 us
  transfers between devices with their start and end apart: 2, of which 2 were waited for; matrix products, arithmetic and copies ran while one was open for 1% of the time, Pallas kernels for 0%

profile of v1, /device:TPU:1, one launch (start us, length us, event | category | flops | bytes accessed | tf_op | source)
XLA Modules:
  0.0 522.3 jit_solution(1734618508663912807)
XLA Ops:
  7.2 0.8 compare_select_fusion.1
  8.0 0.8 compare_and_fusion
  8.8 3.4 gather_fusion
  12.2 0.1 broadcast_select_fusion
  12.2 15.6 %psum.28 = bf16[64,256]{1,0:T(8,128)(2,1)} all-reduce(bf16[64,256]{1,0:T(8,128)(2,1)S(1)} %broadcast_select_fusion), channel_id=1, replica_groups=mesh['loader'=4,'centers'=32] {'loader'}, use_global_device_ids=true, to_apply=%region_0.1 | all-reduce | flops 16384 | bytes 65536 | tf_op jit(solution)/shard_map/psum | solution.py:22
  27.9 0.0 all-reduce.2.cloned.1.call-start
  28.0 0.7 compare_select_fusion
  28.6 3.3 multiply_reduce_fusion.1
  32.0 127.5 %all-gather.2.cloned.1.call-done = bf16[2048,256]{1,0:T(8,128)(2,1)} async-done(((bf16[64,256]{1,0:T(8,128)(2,1)}), bf16[2048,256]{1,0:T(8,128)(2,1)}) %all-gather.2.cloned.1.call-update) | async-done | bytes 1048592 | tf_op jit(solution)/shard_map/all_gather | solution.py:23
  159.5 58.4 %while.12 = (s32[]{:T(128)}, bf16[4,512,8192]{2,1,0:T(8,128)(2,1)}, bf16[4,512,256]{2,1,0:T(8,128)(2,1)}, f32[8192]{0:T(1024)S(1)}, bf16[8192,256]{1,0:T(8,128)(2,1)}, /*index=5*/s32[]{:T(128)}) while((s32[]{:T(128)}, bf16[4,512,8192]{2,1,0:T(8,128)(2,1)}, bf16[4,512,256]{2,1,0:T(8,128)(2,1)}, f32[8192]{0:T(1024)S(1)}, ...), condition=%wide.region_4.5_spmd, body=%wide.region_2.4_spmd.sunk | while | flops 2168847872 | bytes 13145161 | solution.py:33
  159.5 1.2 multiply_reduce_fusion.3
  160.6 13.5 %fusion.22 = bf16[4,512,8192]{2,1,0:T(8,128)(2,1)} fusion(bf16[4,512,8192]{2,1,0:T(8,128)(2,1)} %get-tuple-element.120, s32[]{:T(128)} %get-tuple-element.119, bf16[8192,256]{1,0:T(8,128)(2,1)} %get-tuple-element.129, f32[8192]{0:T(1024)S(1)} %get-tuple-element.128, f32[512]{0:T(512)S(1)} %multiply_reduce_fusion.3, ...), kind=kOutput, calls=%fused_computation.5.clone.1 | convolution fusion | flops 2168455168 | bytes 12880896 | tf_op jit(solution)/shard_map/while/body/eval_jaxpr/dot_general | solution.py:29
  174.1 1.1 multiply_reduce_fusion.3
  175.2 13.5 %fusion.22 = bf16[4,512,8192]{2,1,0:T(8,128)(2,1)} fusion(bf16[4,512,8192]{2,1,0:T(8,128)(2,1)} %get-tuple-element.120, s32[]{:T(128)} %get-tuple-element.119, bf16[8192,256]{1,0:T(8,128)(2,1)} %get-tuple-element.129, f32[8192]{0:T(1024)S(1)} %get-tuple-element.128, f32[512]{0:T(512)S(1)} %multiply_reduce_fusion.3, ...), kind=kOutput, calls=%fused_computation.5.clone.1 | convolution fusion | flops 2168455168 | bytes 12880896 | tf_op jit(solution)/shard_map/while/body/eval_jaxpr/dot_general | solution.py:29
  188.7 1.1 multiply_reduce_fusion.3
  189.8 13.5 %fusion.22 = bf16[4,512,8192]{2,1,0:T(8,128)(2,1)} fusion(bf16[4,512,8192]{2,1,0:T(8,128)(2,1)} %get-tuple-element.120, s32[]{:T(128)} %get-tuple-element.119, bf16[8192,256]{1,0:T(8,128)(2,1)} %get-tuple-element.129, f32[8192]{0:T(1024)S(1)} %get-tuple-element.128, f32[512]{0:T(512)S(1)} %multiply_reduce_fusion.3, ...), kind=kOutput, calls=%fused_computation.5.clone.1 | convolution fusion | flops 2168455168 | bytes 12880896 | tf_op jit(solution)/shard_map/while/body/eval_jaxpr/dot_general | solution.py:29
  203.3 1.1 multiply_reduce_fusion.3
  204.4 13.5 %fusion.22 = bf16[4,512,8192]{2,1,0:T(8,128)(2,1)} fusion(bf16[4,512,8192]{2,1,0:T(8,128)(2,1)} %get-tuple-element.120, s32[]{:T(128)} %get-tuple-element.119, bf16[8192,256]{1,0:T(8,128)(2,1)} %get-tuple-element.129, f32[8192]{0:T(1024)S(1)} %get-tuple-element.128, f32[512]{0:T(512)S(1)} %multiply_reduce_fusion.3, ...), kind=kOutput, calls=%fused_computation.5.clone.1 | convolution fusion | flops 2168455168 | bytes 12880896 | tf_op jit(solution)/shard_map/while/body/eval_jaxpr/dot_general | solution.py:29
  217.9 15.7 %convolution_bitcast_fusion = f32[16,2048]{1,0:T(8,128)} fusion(bf16[2048,8192]{1,0:T(8,128)(2,1)} %bitcast.28, f32[16,8192]{1,0:T(8,128)S(1)} %copy-done.1), kind=kOutput, calls=%fused_computation.11 | convolution fusion | flops 537001984 | bytes 34209792 | tf_op jit(solution)/shard_map/dot_general | solution.py:36
  233.6 161.8 %all-reduce.2.cloned.1.call-done = f32[16,2048]{1,0:T(8,128)} async-done(((f32[16,2048]{1,0:T(8,128)}), f32[16,2048]{1,0:T(8,128)}) %all-reduce.2.cloned.1.call-update) | async-done | bytes 131088 | tf_op jit(solution)/shard_map/psum | solution.py:39
  395.4 14.8 %multiply_subtract_fusion = (f32[16,8192]{1,0:T(8,128)S(1)}, f32[16,8192]{1,0:T(8,128)S(1)}) fusion(f32[16,8192]{1,0:T(8,128)S(1)} %copy-done.1, bf16[2048,8192]{1,0:T(8,128)(2,1)} %bitcast.29, f32[16,2048]{1,0:T(8,128)} %all-reduce.2.cloned.1.call-done, f32[16,2048]{1,0:T(8,128)S(1)} %copy-done.3), kind=kOutput, calls=%fused_computation.14 | convolution fusion | flops 537198592 | bytes 35389440 | tf_op jit(solution)/shard_map/dot_general | solution.py:41
  410.3 2.6 copy.10
  412.9 2.8 gather_fusion.1
  415.7 0.2 fusion.10
  415.9 66.8 %psum.30 = f32[16,128]{1,0:T(8,128)S(1)} all-reduce(f32[16,128]{1,0:T(8,128)S(1)} %fusion.10), channel_id=1, replica_groups=mesh['loader'=4,'centers'=32] {'centers'}, use_global_device_ids=true, to_apply=%region_6.7 | all-reduce | flops 2048 | bytes 16384 | tf_op jit(solution)/shard_map/psum | solution.py:46
  482.6 20.8 %psum.31 = f32[16,128]{1,0:T(8,128)S(1)} all-reduce(f32[16,128]{1,0:T(8,128)S(1)} %psum.30), channel_id=1, replica_groups=mesh['loader'=4,'centers'=32] {'loader'}, use_global_device_ids=true, to_apply=%region_7.8 | all-reduce | flops 2048 | bytes 16384 | tf_op jit(solution)/shard_map/psum | solution.py:46
  503.5 0.1 fusion.5
  503.6 0.1 copy.12
  503.7 2.6 copy.11
  506.3 4.9 scatter_fusion
  511.3 3.5 copy.13
  514.8 0.7 copy.25
  (16 shorter events, 0.1 us)
Async XLA Ops:
  7.2 408.5 %copy-start = (f32[64,128]{1,0:T(8,128)S(1)}, f32[64,128]{1,0:T(8,128)}, u32[]{:S(2)}) copy-start(f32[64,128]{1,0:T(8,128)} %param.16) | copy-start | bytes 98308
  7.2 152.3 %all-gather.2.cloned.1.call-start = ((), (), s32[]{:S(2)}) async-start(), calls=%async_computation | async-start | bytes 1081344 | tf_op jit(solution)/shard_map/all_gather | solution.py:23
  27.9 367.5 %all-reduce.2.cloned.1.call-start = ((), (), s32[]{:S(2)}) async-start(), calls=%async_computation.1 | async-start | bytes 262144 | tf_op jit(solution)/shard_map/psum | solution.py:39
  159.5 58.4 %copy-start.1 = (f32[16,8192]{1,0:T(8,128)S(1)}, f32[16,8192]{1,0:T(8,128)}, u32[]{:S(2)}) copy-start(f32[16,8192]{1,0:T(8,128)} %param.14) | copy-start | bytes 1572868
  217.9 177.5 %copy-start.3 = (f32[16,2048]{1,0:T(8,128)S(1)}, f32[16,2048]{1,0:T(8,128)}, u32[]{:S(2)}) copy-start(f32[16,2048]{1,0:T(8,128)} %param.12) | copy-start | bytes 393220
  233.6 269.9 %copy-start.4 = (f32[128]{0:T(128)S(1)}, f32[128]{0:T(128)}, u32[]{:S(2)}) copy-start(f32[128]{0:T(128)} %param.17) | copy-start | bytes 1540
  395.4 119.3 %copy-start.2 = (f32[16,2048]{1,0:T(8,128)S(1)}, f32[16,2048]{1,0:T(8,128)}, u32[]{:S(2)}) copy-start(f32[16,2048]{1,0:T(8,128)} %all-reduce.2.cloned.1.call-done) | copy-start | bytes 393220
Sparse Core Ops, SparseCore 0:
  28.0 131.4 all-gather.1
  233.7 161.6 all-reduce.1
